TPU v7x, 128 devices: a whole 4x4x4 slice. The times are simulated.
128 devices in a mesh: leaf: 8 (over y, core), front: 16 (over x, z).
Axes of the slice: x: 4, y: 4, z: 4, core: 2. Of those that a mesh axis runs over, the one named last changes fastest.
Arguments:
- inv_factors: bfloat16 [8, 2, 1024, 1024], P('leaf', None, 'front')
- panel_rows: bfloat16 [8, 1024, 1024], P('leaf', 'front'), may hold values from -6 to 6
- border: bfloat16 [8, 2048, 2048], P('leaf', 'front'), may hold values from -6 to 6
- tail: bfloat16 [8, 2048, 2048], P('leaf', 'front'), may hold values from -6 to 6
- front_sizes: int32 [8], replicated, may hold values from 1024 to 2048, as said below
- block_map: int32 [8, 16], replicated, may hold values from 0 to 31, as said below
- block_owner: int32 [8, 32], replicated, may hold values from 0 to 47, as said below
Outputs:
- link_factor: bfloat16 [8, 1024, 1024], P('leaf', 'front')
- border_factor: bfloat16 [8, 2048, 2048], P('leaf', 'front')
- parent_update: float32 [8, 4096, 6144], P('leaf', None, 'front')
Inputs may be any that keep to these rules, and one draw needn't show every extreme that they name: `front_sizes`: the live rows of some child always equal 2048; every child has at least 1024. `block_map`: the entries of one child's row are distinct. `block_owner`: the entries of one parent's row are distinct; slot s belongs to front index s // 3, so no front index owns more than 3 blocks of a parent, and in every parent's row one front index owns exactly 3.
All inputs are finite; a program needn't handle non-finite values.
Results may differ from a plain program's by a relative error of at most 0.0055.
Values may be sent and summed in bfloat16 or wider, within the bound.
No kernel may reach another device: no remote copies, remote signals or barrier semaphores. Data moves between devices by JAX's collectives and lax.ppermute only.
A program may use at most 64 MiB of HBM per device.

v0:
```python
import jax
import jax.numpy as jnp
from jax import lax
from jax.sharding import PartitionSpec as P

PANEL = 1024
BLOCK = 128
SLOTS = 3


def passed_along(value, axis, by):
    devices = lax.axis_size(axis)
    return lax.ppermute(value, axis, [(i, (i + by) % devices) for i in range(devices)])


def dot_rows(left_rows, right_rows):
    return lax.dot_general(
        left_rows, right_rows, (((1,), (1,)), ((), ())), preferred_element_type=jnp.float32
    )


def against(left_rows, piece):
    return dot_rows(left_rows, piece)


def pick_row(table, index):
    chooser = (jnp.arange(table.shape[0], dtype=jnp.int32)[:, None] == index).astype(jnp.int32)
    return jnp.sum(chooser * table, axis=0)


def route_tiles(contribution, owner_line, child_map, nfront, parent_blocks):
    block_pick = (child_map[:, None] == jnp.arange(parent_blocks, dtype=jnp.int32)[None, :]).astype(
        jnp.int32
    )
    slot_index = jnp.sum(block_pick * owner_line[None, :], axis=1)
    owner_front = slot_index // SLOTS
    owner_slot = slot_index % SLOTS
    select = (jnp.arange(nfront, dtype=jnp.int32)[:, None, None] == owner_front[None, None, :]) & (
        jnp.arange(SLOTS, dtype=jnp.int32)[None, :, None] == owner_slot[None, None, :]
    )
    tiles = contribution.reshape(BLOCK, nfront, BLOCK)
    return jnp.einsum(
        "ocb,rbd->orcd", select.astype(jnp.bfloat16), tiles, preferred_element_type=jnp.float32
    ).astype(jnp.bfloat16)


def place_rows(arrived, child_map, nfront, parent_blocks):
    row_hot = (jnp.arange(parent_blocks, dtype=jnp.int32)[:, None] == child_map[None, :]).astype(
        jnp.bfloat16
    )
    merged = jnp.dot(
        row_hot, arrived.reshape(nfront, BLOCK * SLOTS * BLOCK), preferred_element_type=jnp.float32
    )
    return merged.reshape(parent_blocks * BLOCK, SLOTS * BLOCK)


def per_device(inv_factors, panel_rows, border, tail, front_sizes, block_map, block_owner):
    nfront = lax.axis_size("front")
    nleaf = lax.axis_size("leaf")
    half_leaf = nleaf // 2
    leaf_group = lax.axis_index("leaf")
    front_place = lax.axis_index("front")
    first_inv = inv_factors[0, 0]
    second_inv = inv_factors[0, 1]
    upper_rows = panel_rows[0]
    left_cols = border[0, :, :PANEL]
    right_cols = border[0, :, PANEL:]
    stacked = jnp.concatenate([upper_rows, left_cols], axis=0)
    upper_count = upper_rows.shape[0]
    projected = against(stacked, lax.all_gather(first_inv, "front", axis=0, tiled=True))
    projected = projected.astype(jnp.bfloat16)
    link_local = projected[:upper_count]
    first_local = projected[upper_count:]
    coupled = against(first_local, lax.all_gather(link_local, "front", axis=0, tiled=True))
    updated = (right_cols.astype(jnp.float32) - coupled).astype(jnp.bfloat16)
    second_local = against(updated, lax.all_gather(second_inv, "front", axis=0, tiled=True))
    second_local = second_local.astype(jnp.bfloat16)
    factor_local = jnp.concatenate([first_local, second_local], axis=1)
    schur = tail[0].astype(jnp.float32) - against(
        factor_local, lax.all_gather(factor_local, "front", axis=0, tiled=True)
    )
    contrib_rows = BLOCK * nfront
    live = front_sizes[leaf_group]
    row_global = front_place * BLOCK + jnp.arange(BLOCK, dtype=jnp.int32)
    col_global = jnp.arange(contrib_rows, dtype=jnp.int32)
    keep = (row_global[:, None] < live) & (col_global[None, :] < live)
    contribution = jnp.where(keep, schur, jnp.float32(0.0)).astype(jnp.bfloat16)
    parent_blocks = 2 * nfront
    parent_group = (leaf_group + half_leaf) % nleaf
    child_group = (leaf_group + nleaf - half_leaf) % nleaf
    child_map_here = pick_row(block_map, child_group)
    own_map = pick_row(block_map, leaf_group)
    routed = route_tiles(
        contribution, pick_row(block_owner, parent_group), own_map, nfront, parent_blocks
    )
    sorted_tiles = lax.all_to_all(routed, "front", split_axis=0, concat_axis=0, tiled=True)
    arrived = passed_along(sorted_tiles, "leaf", half_leaf)
    merged = place_rows(arrived, child_map_here, nfront, parent_blocks)
    return (link_local[None], factor_local[None], merged[None])


def solution(mesh):
    return jax.shard_map(
        per_device,
        mesh=mesh,
        in_specs=(
            P("leaf", None, "front", None),
            P("leaf", "front", None),
            P("leaf", "front", None),
            P("leaf", "front", None),
            P(),
            P(),
            P(),
        ),
        out_specs=(P("leaf", "front", None), P("leaf", "front", None), P("leaf", None, "front")),
        check_vma=False,
    )
```

profile of v0, /device:TPU:0, one launch (start us, length us, event | category | flops | bytes accessed | tf_op | source)
XLA Modules:
  0.0 320.9 jit_solution(9470419997501196426)
XLA Ops:
  7.2 0.0 all-gather.11.cloned.1.call-start
  7.2 1.7 fusion.33
  8.9 0.0 all-gather.11.cloned.1.call-update
  8.9 0.0 all-gather.13.cloned.1.call-start
  9.0 0.7 all-gather.13.cloned.1.call-update
  9.7 0.0 all-gather.7.cloned.1.call-start
  9.7 1.0 slice_bitcast_fusion
  10.7 0.0 copy-start.1
  10.7 47.8 %all-gather.11.cloned.1.call-done = bf16[1,1,1024,1024]{3,2,1,0:T(8,128)(2,1)} async-done(((bf16[1,1,64,1024]{3,2,1,0:T(8,128)(2,1)}), bf16[1,1,1024,1024]{3,2,1,0:T(8,128)(2,1)}) %all-gather.11.cloned.1.call-update) | async-done | bytes 2097168 | tf_op jit(solution)/shard_map/all_gather | solution.py:70
  58.5 2.5 fusion.7
  61.0 0.7 fusion.32
  61.7 0.0 all-gather.7.cloned.1.call-update
  61.7 0.0 all-gather.9.cloned.1.call-start
  61.8 43.9 %all-gather.13.cloned.1.call-done = bf16[1,1,1024,1024]{3,2,1,0:T(8,128)(2,1)} async-done(((bf16[1,1,64,1024]{3,2,1,0:T(8,128)(2,1)}), bf16[1,1,1024,1024]{3,2,1,0:T(8,128)(2,1)}) %all-gather.13.cloned.1.call-update) | async-done | bytes 2097168 | tf_op jit(solution)/shard_map/all_gather | solution.py:76
  105.7 47.3 %all-gather.7.cloned.1.call-done = bf16[1024,1024]{1,0:T(8,128)(2,1)} async-done(((bf16[64,1024]{1,0:T(8,128)(2,1)}), bf16[1024,1024]{1,0:T(8,128)(2,1)}) %all-gather.7.cloned.1.call-update) | async-done | bytes 2097168 | tf_op jit(solution)/shard_map/all_gather | solution.py:74
  153.0 0.0 copy-done.1
  153.0 3.7 %fusion.11 = bf16[128,1024]{1,0:T(8,128)(2,1)S(1)} fusion(bf16[1,1,1024,1024]{3,2,1,0:T(8,128)(2,1)} %all-gather.13.cloned.1.call-done, bf16[1024,1024]{1,0:T(8,128)(2,1)} %all-gather.7.cloned.1.call-done, bf16[1,128,2048]{2,1,0:T(8,128)(2,1)S(1)} %copy-done.1, bf16[192,1024]{1,0:T(8,128)(2,1)S(1)} %fusion.7), kind=kOutput, calls=%fused_computation.12 | convolution fusion | flops 537395200 | bytes 4980736 | tf_op jit(solution)/shard_map/dot_general | solution.py:17
  156.8 0.0 copy-start.4
  156.8 0.0 copy-start.2
  156.8 0.0 copy-start.3
  156.8 0.0 copy-start
  156.8 1.1 pad_maximum_fusion
  157.9 0.0 all-gather.9.cloned.1.call-update
  158.0 0.0 copy-done.4
  158.0 0.7 dynamic_slice.3
  158.6 0.7 add_compare_fusion
  159.3 0.7 iota_compare_fusion.4
  160.0 0.0 copy-done.2
  160.1 0.1 multiply_reduce_fusion
  160.1 0.0 copy-done.3
  160.1 0.1 multiply_reduce_fusion.2
  160.2 0.2 select_reduce_fusion
  160.5 67.8 %all-gather.9.cloned.1.call-done = bf16[2048,2048]{1,0:T(8,128)(2,1)} async-done(((bf16[128,2048]{1,0:T(8,128)(2,1)}), bf16[2048,2048]{1,0:T(8,128)(2,1)}) %all-gather.9.cloned.1.call-update) | async-done | bytes 8388624 | tf_op jit(solution)/shard_map/all_gather | solution.py:80
  228.2 0.0 copy-done
  228.2 6.3 %fusion.10 = bf16[16,8,16,128]{3,1,2,0:T(8,128)(2,1)S(1)} fusion(bf16[2048,2048]{1,0:T(8,128)(2,1)} %all-gather.9.cloned.1.call-done, bf16[1,128,2048]{2,1,0:T(8,128)(2,1)S(1)} %copy-done, pred[2048]{0:T(1024)(128)(4,1)S(1)} %iota_compare_fusion.4, pred[128]{0:T(512)(128)(4,1)S(1)} %add_compare_fusion, bf16[128,1024]{1,0:T(8,128)(2,1)S(1)} %fusion.11, ...), kind=kOutput, calls=%fused_computation.11 | convolution fusion | flops 1076101120 | bytes 9963648 | tf_op jit(solution)/shard_map/dot_general | solution.py:17
  234.5 0.1 copy.17
  234.7 0.5 fusion.6
  235.2 0.4 copy.14
  235.6 27.6 %all_to_all.5 = bf16[16,128,3,128]{3,1,2,0:T(8,128)(2,1)S(1)} all-to-all(bf16[16,128,3,128]{3,1,2,0:T(8,128)(2,1)S(1)} %copy.14), channel_id=1, replica_groups=mesh['leaf'=8,'front'=16] {'front'}, dimensions={0} | all-to-all | bytes 3145728 | tf_op jit(solution)/shard_map/all_to_all | solution.py:96
  263.2 3.0 collective-permute-start
  266.2 33.3 %collective-permute-done = bf16[16,128,3,128]{3,1,2,0:T(8,128)(2,1)S(1)} collective-permute-done((bf16[16,128,3,128]{3,1,2,0:T(8,128)(2,1)S(1)}, bf16[16,128,3,128]{3,1,2,0:T(8,128)(2,1)S(1)}, u32[]{:S(2)}, u32[]{:S(2)}) %collective-permute-start) | collective-permute-done | bytes 1572896 | tf_op jit(solution)/shard_map/ppermute | solution.py:13
  299.5 1.4 copy.15
  300.9 2.4 reshape.114
  303.3 5.0 %fusion.24 = f32[32,49152]{1,0:T(8,128)} fusion(bf16[16,49152]{1,0:T(8,128)(2,1)} %reshape.114, s32[16]{0:T(128)S(1)} %get-tuple-element.3), kind=kOutput, calls=%fused_computation.26 | convolution fusion | flops 50332160 | bytes 7864384 | tf_op jit(solution)/shard_map/dot_general | solution.py:51
  308.3 6.1 %broadcast_in_dim_reshape.3 = f32[1,4096,384]{2,1,0:T(8,128)} reshape(f32[32,49152]{1,0:T(8,128)} %fusion.24) | data formatting | bytes 12582912 | tf_op jit(solution)/shard_map/broadcast_in_dim;reshape | solution.py:99
  (5 shorter events, 0.1 us)
Async XLA Ops:
  7.2 51.3 %all-gather.11.cloned.1.call-start = ((), (), s32[]{:S(2)}) async-start(), calls=%async_computation.3 | async-start | bytes 2228224 | tf_op jit(solution)/shard_map/all_gather | solution.py:70
  8.9 96.8 %all-gather.13.cloned.1.call-start = ((), (), s32[]{:S(2)}) async-start(), calls=%async_computation.4 | async-start | bytes 2228224 | tf_op jit(solution)/shard_map/all_gather | solution.py:76
  9.7 143.4 %all-gather.7.cloned.1.call-start = ((), (), s32[]{:S(2)}) async-start(), calls=%async_computation.1 | async-start | bytes 2228224 | tf_op jit(solution)/shard_map/all_gather | solution.py:74
  10.7 142.3 %copy-start.1 = (bf16[1,128,2048]{2,1,0:T(8,128)(2,1)S(1)}, bf16[1,128,2048]{2,1,0:T(8,128)(2,1)}, u32[]{:S(2)}) copy-start(bf16[1,128,2048]{2,1,0:T(8,128)(2,1)} %param.9) | copy-start | bytes 1572868
  61.7 166.5 %all-gather.9.cloned.1.call-start = ((), (), s32[]{:S(2)}) async-start(), calls=%async_computation.2 | async-start | bytes 8912896 | tf_op jit(solution)/shard_map/all_gather | solution.py:80
  156.8 1.2 copy-start.4
  156.8 3.3 %copy-start.2 = (s32[8,32]{1,0:T(8,128)S(1)}, s32[8,32]{1,0:T(8,128)}, u32[]{:S(2)}) copy-start(s32[8,32]{1,0:T(8,128)} %param.13) | copy-start | bytes 3076
  156.8 3.3 %copy-start.3 = (s32[8,16]{1,0:T(8,128)S(1)}, s32[8,16]{1,0:T(8,128)}, u32[]{:S(2)}) copy-start(s32[8,16]{1,0:T(8,128)} %param.12) | copy-start | bytes 1540
  156.8 71.4 %copy-start = (bf16[1,128,2048]{2,1,0:T(8,128)(2,1)S(1)}, bf16[1,128,2048]{2,1,0:T(8,128)(2,1)}, u32[]{:S(2)}) copy-start(bf16[1,128,2048]{2,1,0:T(8,128)(2,1)} %param.10) | copy-start | bytes 1572868
  263.2 36.3 %collective-permute-start = (bf16[16,128,3,128]{3,1,2,0:T(8,128)(2,1)S(1)}, bf16[16,128,3,128]{3,1,2,0:T(8,128)(2,1)S(1)}, u32[]{:S(2)}, u32[]{:S(2)}) collective-permute-start(bf16[16,128,3,128]{3,1,2,0:T(8,128)(2,1)S(1)} %all_to_all.5), channel_id=1, source_target_pairs={{0,64},{16,80},{32,96},{48,112},{64,0},{80,16},{96,32},{112,48},{1... | collective-permute-start | bytes 4718600 | tf_op jit(solution)/shard_map/ppermute | solution.py:13
Sparse Core Ops, SparseCore 0:
  10.7 47.7 all-gather.10
  61.2 44.5 all-gather.12
  108.5 44.5 all-gather.6
  158.1 70.1 all-gather.8
where the time goes:
time: 321 us
  waiting for transfers between devices  241 us (75%)
  blocking collectives  27.6 us (9%)
  matrix products  18.1 us (6%)
  local copies, waits for them, and re-layouts  14.5 us (5%)
  between operations  13.9 us (4%)
    all_gather x1, waiting for transfers between devices, per_device(): lax.all_gather(factor_local, 'front', axis=0, tiled=True)  67.8 us
    all_gather x1, waiting for transfers between devices, per_device(): lax.all_gather(first_inv, 'front', axis=0, tiled=True)  47.8 us
    all_gather x1, waiting for transfers between devices, per_device(): lax.all_gather(link_local, 'front', axis=0, tiled=True)  47.3 us
    all_gather x1, waiting for transfers between devices, per_device(): lax.all_gather(second_inv, 'front', axis=0, tiled=True)  43.9 us
    ppermute x1, waiting for transfers between devices, passed_along(): lax.ppermute(value, axis, [(i, (i + by) % devices) for i in range(devices)])  33.3 us
    all_to_all x1, blocking collectives, per_device(): lax.all_to_all(routed, 'front', split_axis=0, concat_axis=0, tiled=True)  27.6 us
    dot_general x3, matrix products, dot_rows(): lax.dot_general(left_rows, right_rows, (((1,), (1,)), ((), ())), preferre...  12.6 us
  transfers between devices with their start and end apart: 5, of which 5 were waited for; matrix products, arithmetic and copies ran while one was open for 2% of the time, Pallas kernels for 0%

commit v1 on v0

--- a/solution.py
+++ b/solution.py
@@ -67,7 +67,12 @@
     right_cols = border[0, :, PANEL:]
     stacked = jnp.concatenate([upper_rows, left_cols], axis=0)
     upper_count = upper_rows.shape[0]
-    projected = against(stacked, lax.all_gather(first_inv, "front", axis=0, tiled=True))
+    projected = against(
+        stacked,
+        jnp.concatenate(
+            lax.all_to_all(jnp.stack([first_inv] * lax.axis_size("front")), "front", 0, 0), axis=0
+        ),
+    )
     projected = projected.astype(jnp.bfloat16)
     link_local = projected[:upper_count]
     first_local = projected[upper_count:]

time: 321 us -> 288 us (0.90)
  waiting for transfers between devices: 241 us -> 201 us
  starting transfers between devices: 3.17 us -> 11.2 us
    all_gather x1 -> x0, waiting for transfers between devices: 47.8 us -> none  [per_device(): lax.all_gather(first_inv, 'front', axis=0, tiled=True)]
    all_to_all x0 -> x1, waiting for transfers between devices: none -> 32.3 us  [per_device(): lax.all_to_all(jnp.stack([first_inv] * lax.axis_size('front')), 'front',...]
    all_gather x1, waiting for transfers between devices: 43.9 us -> 20.2 us  [per_device(): lax.all_gather(second_inv, 'front', axis=0, tiled=True)]
    all_to_all x0 -> x1, starting transfers between devices: none -> 8.12 us  [per_device(): lax.all_to_all(jnp.stack([first_inv] * lax.axis_size('front')), 'front',...]
where the time goes in v1:
time: 288 us
  waiting for transfers between devices  201 us (70%)
  blocking collectives  27.6 us (10%)
  matrix products  16.4 us (6%)
  local copies, waits for them, and re-layouts  15.1 us (5%)
  between operations  13.9 us (5%)
  starting transfers between devices  11.2 us (4%)
    all_gather x1, waiting for transfers between devices, per_device(): lax.all_gather(factor_local, 'front', axis=0, tiled=True)  67.8 us
    all_gather x1, waiting for transfers between devices, per_device(): lax.all_gather(link_local, 'front', axis=0, tiled=True)  47.3 us
    ppermute x1, waiting for transfers between devices, passed_along(): lax.ppermute(value, axis, [(i, (i + by) % devices) for i in range(devices)])  33.3 us
    all_to_all x1, waiting for transfers between devices, per_device(): lax.all_to_all(jnp.stack([first_inv] * lax.axis_size('front')), 'front',...  32.3 us
    all_to_all x1, blocking collectives, per_device(): lax.all_to_all(routed, 'front', split_axis=0, concat_axis=0, tiled=True)  27.6 us
    all_gather x1, waiting for transfers between devices, per_device(): lax.all_gather(second_inv, 'front', axis=0, tiled=True)  20.2 us
    dot_general x3, matrix products, dot_rows(): lax.dot_general(left_rows, right_rows, (((1,), (1,)), ((), ())), preferre...  10.9 us
    all_to_all x1, starting transfers between devices, per_device(): lax.all_to_all(jnp.stack([first_inv] * lax.axis_size('front')), 'front',...  8.12 us
  transfers between devices with their start and end apart: 5, of which 5 were waited for; matrix products, arithmetic and copies ran while one was open for 2% of the time, Pallas kernels for 0%

profile of v1, /device:TPU:0, one launch (start us, length us, event | category | flops | bytes accessed | tf_op | source)
XLA Modules:
  0.0 288.0 jit_solution(10922062571506478428)
XLA Ops:
  7.2 0.0 all-gather.9.cloned.1.call-start
  7.2 1.6 fusion.28
  8.9 0.0 all-gather.9.cloned.1.call-update
  8.9 1.6 stack.3
  10.5 0.0 copy-start.1
  10.5 0.0 copy-start.4
  10.5 8.1 %all-to-all-start = ((bf16[16,64,1024]{2,1,0:T(8,128)(2,1)}), bf16[16,64,1024]{2,1,0:T(8,128)(2,1)S(1)}, u32[]{:S(2)}, u32[]{:S(2)}) async-start(bf16[16,64,1024]{2,1,0:T(8,128)(2,1)} %stack.3), calls=%async_computation | async-start | bytes 4194304 | tf_op jit(solution)/shard_map/all_to_all | solution.py:73
  18.6 0.0 all-gather.5.cloned.1.call-start
  18.6 0.0 copy-done.1
  18.7 32.3 %all-to-all-done = bf16[16,64,1024]{2,1,0:T(8,128)(2,1)S(1)} async-done(((bf16[16,64,1024]{2,1,0:T(8,128)(2,1)}), bf16[16,64,1024]{2,1,0:T(8,128)(2,1)S(1)}, u32[]{:S(2)}, u32[]{:S(2)}) %all-to-all-start) | async-done | bytes 2097184 | tf_op jit(solution)/shard_map/all_to_all | solution.py:73
  51.0 0.0 copy-done.4
  51.0 0.8 convolution_convert_fusion.1
  51.8 0.7 fusion.27
  52.5 0.0 all-gather.5.cloned.1.call-update
  52.6 0.0 all-gather.7.cloned.1.call-start
  52.6 20.2 %all-gather.9.cloned.1.call-done = bf16[1,1,1024,1024]{3,2,1,0:T(8,128)(2,1)} async-done(((bf16[1,1,64,1024]{3,2,1,0:T(8,128)(2,1)}), bf16[1,1,1024,1024]{3,2,1,0:T(8,128)(2,1)}) %all-gather.9.cloned.1.call-update) | async-done | bytes 2097168 | tf_op jit(solution)/shard_map/all_gather | solution.py:81
  72.8 47.3 %all-gather.5.cloned.1.call-done = bf16[1024,1024]{1,0:T(8,128)(2,1)} async-done(((bf16[64,1024]{1,0:T(8,128)(2,1)}), bf16[1024,1024]{1,0:T(8,128)(2,1)}) %all-gather.5.cloned.1.call-update) | async-done | bytes 2097168 | tf_op jit(solution)/shard_map/all_gather | solution.py:79
  120.1 3.7 %fusion.6 = bf16[128,1024]{1,0:T(8,128)(2,1)S(1)} fusion(bf16[1,1,1024,1024]{3,2,1,0:T(8,128)(2,1)} %all-gather.9.cloned.1.call-done, bf16[1024,1024]{1,0:T(8,128)(2,1)} %all-gather.5.cloned.1.call-done, bf16[1,128,2048]{2,1,0:T(8,128)(2,1)S(1)} %copy-done.1, bf16[192,1024]{1,0:T(8,128)(2,1)S(1)} %convolution_convert_fusion.1), kind=kOutput, calls=%fused_computation.10 | convolution fusion | flops 537395200 | bytes 4980736 | tf_op jit(solution)/shard_map/dot_general | solution.py:17
  123.8 0.0 copy-start.5
  123.9 0.0 copy-start.2
  123.9 0.0 copy-start.3
  123.9 0.0 copy-start
  123.9 1.1 pad_maximum_fusion
  125.0 0.0 all-gather.7.cloned.1.call-update
  125.0 0.0 copy-done.5
  125.0 0.7 dynamic_slice.3
  125.7 0.7 add_compare_fusion
  126.4 0.7 iota_compare_fusion.4
  127.1 0.0 copy-done.2
  127.1 0.1 multiply_reduce_fusion
  127.2 0.0 copy-done.3
  127.2 0.1 multiply_reduce_fusion.2
  127.3 0.2 select_reduce_fusion
  127.5 67.8 %all-gather.7.cloned.1.call-done = bf16[2048,2048]{1,0:T(8,128)(2,1)} async-done(((bf16[128,2048]{1,0:T(8,128)(2,1)}), bf16[2048,2048]{1,0:T(8,128)(2,1)}) %all-gather.7.cloned.1.call-update) | async-done | bytes 8388624 | tf_op jit(solution)/shard_map/all_gather | solution.py:85
  195.3 0.0 copy-done
  195.3 6.3 %fusion.5 = bf16[16,8,16,128]{3,1,2,0:T(8,128)(2,1)S(1)} fusion(bf16[2048,2048]{1,0:T(8,128)(2,1)} %all-gather.7.cloned.1.call-done, bf16[1,128,2048]{2,1,0:T(8,128)(2,1)S(1)} %copy-done, pred[2048]{0:T(1024)(128)(4,1)S(1)} %iota_compare_fusion.4, pred[128]{0:T(512)(128)(4,1)S(1)} %add_compare_fusion, bf16[128,1024]{1,0:T(8,128)(2,1)S(1)} %fusion.6, ...), kind=kOutput, calls=%fused_computation.9 | convolution fusion | flops 1076101120 | bytes 9963648 | tf_op jit(solution)/shard_map/dot_general | solution.py:17
  201.6 0.1 copy.17
  201.7 0.5 fusion.4
  202.3 0.4 copy.14
  202.7 27.6 %all_to_all.10 = bf16[16,128,3,128]{3,1,2,0:T(8,128)(2,1)S(1)} all-to-all(bf16[16,128,3,128]{3,1,2,0:T(8,128)(2,1)S(1)} %copy.14), channel_id=1, replica_groups=mesh['leaf'=8,'front'=16] {'front'}, dimensions={0} | all-to-all | bytes 3145728 | tf_op jit(solution)/shard_map/all_to_all | solution.py:101
  230.3 3.0 %collective-permute-start = (bf16[16,128,3,128]{3,1,2,0:T(8,128)(2,1)S(1)}, bf16[16,128,3,128]{3,1,2,0:T(8,128)(2,1)S(1)}, u32[]{:S(2)}, u32[]{:S(2)}) collective-permute-start(bf16[16,128,3,128]{3,1,2,0:T(8,128)(2,1)S(1)} %all_to_all.10), channel_id=1, source_target_pairs={{0,64},{16,80},{32,96},{48,112},{64,0},{80,16},{96,32},{112,48},{1... | collective-permute-start | bytes 4718600 | tf_op jit(solution)/shard_map/ppermute | solution.py:13
  233.3 33.3 %collective-permute-done = bf16[16,128,3,128]{3,1,2,0:T(8,128)(2,1)S(1)} collective-permute-done((bf16[16,128,3,128]{3,1,2,0:T(8,128)(2,1)S(1)}, bf16[16,128,3,128]{3,1,2,0:T(8,128)(2,1)S(1)}, u32[]{:S(2)}, u32[]{:S(2)}) %collective-permute-start) | collective-permute-done | bytes 1572896 | tf_op jit(solution)/shard_map/ppermute | solution.py:13
  266.6 1.4 copy.15
  268.0 2.4 reshape.120
  270.3 5.0 %fusion.19 = f32[32,49152]{1,0:T(8,128)} fusion(bf16[16,49152]{1,0:T(8,128)(2,1)} %reshape.120, s32[16]{0:T(128)S(1)} %get-tuple-element.3), kind=kOutput, calls=%fused_computation.25 | convolution fusion | flops 50332160 | bytes 7864384 | tf_op jit(solution)/shard_map/dot_general | solution.py:51
  275.3 6.1 %broadcast_in_dim_reshape.3 = f32[1,4096,384]{2,1,0:T(8,128)} reshape(f32[32,49152]{1,0:T(8,128)} %fusion.19) | data formatting | bytes 12582912 | tf_op jit(solution)/shard_map/broadcast_in_dim;reshape | solution.py:104
  (6 shorter events, 0.1 us)
Async XLA Ops:
  7.2 65.7 %all-gather.9.cloned.1.call-start = ((), (), s32[]{:S(2)}) async-start(), calls=%async_computation.4 | async-start | bytes 2228224 | tf_op jit(solution)/shard_map/all_gather | solution.py:81
  10.5 8.2 %copy-start.1 = (bf16[1,128,2048]{2,1,0:T(8,128)(2,1)S(1)}, bf16[1,128,2048]{2,1,0:T(8,128)(2,1)}, u32[]{:S(2)}) copy-start(bf16[1,128,2048]{2,1,0:T(8,128)(2,1)} %param.9) | copy-start | bytes 1572868
  10.5 40.5 %copy-start.4 = (bf16[1,64,1024]{2,1,0:T(8,128)(2,1)S(1)}, bf16[1,64,1024]{2,1,0:T(8,128)(2,1)}, u32[]{:S(2)}) copy-start(bf16[1,64,1024]{2,1,0:T(8,128)(2,1)} %param.8) | copy-start | bytes 393220
  10.5 40.5 %all-to-all-start = ((bf16[16,64,1024]{2,1,0:T(8,128)(2,1)}), bf16[16,64,1024]{2,1,0:T(8,128)(2,1)S(1)}, u32[]{:S(2)}, u32[]{:S(2)}) async-start(bf16[16,64,1024]{2,1,0:T(8,128)(2,1)} %stack.3), calls=%async_computation | async-start | bytes 4194304 | tf_op jit(solution)/shard_map/all_to_all | solution.py:73
  18.6 101.5 %all-gather.5.cloned.1.call-start = ((), (), s32[]{:S(2)}) async-start(), calls=%async_computation.2 | async-start | bytes 2228224 | tf_op jit(solution)/shard_map/all_gather | solution.py:79
  52.6 142.7 %all-gather.7.cloned.1.call-start = ((), (), s32[]{:S(2)}) async-start(), calls=%async_computation.3 | async-start | bytes 8912896 | tf_op jit(solution)/shard_map/all_gather | solution.py:85
  123.8 1.2 copy-start.5
  123.9 3.3 %copy-start.2 = (s32[8,32]{1,0:T(8,128)S(1)}, s32[8,32]{1,0:T(8,128)}, u32[]{:S(2)}) copy-start(s32[8,32]{1,0:T(8,128)} %param.13) | copy-start | bytes 3076
  123.9 3.3 %copy-start.3 = (s32[8,16]{1,0:T(8,128)S(1)}, s32[8,16]{1,0:T(8,128)}, u32[]{:S(2)}) copy-start(s32[8,16]{1,0:T(8,128)} %param.12) | copy-start | bytes 1540
  123.9 71.4 %copy-start = (bf16[1,128,2048]{2,1,0:T(8,128)(2,1)S(1)}, bf16[1,128,2048]{2,1,0:T(8,128)(2,1)}, u32[]{:S(2)}) copy-start(bf16[1,128,2048]{2,1,0:T(8,128)(2,1)} %param.10) | copy-start | bytes 1572868
  230.3 36.3 %collective-permute-start = (bf16[16,128,3,128]{3,1,2,0:T(8,128)(2,1)S(1)}, bf16[16,128,3,128]{3,1,2,0:T(8,128)(2,1)S(1)}, u32[]{:S(2)}, u32[]{:S(2)}) collective-permute-start(bf16[16,128,3,128]{3,1,2,0:T(8,128)(2,1)S(1)} %all_to_all.10), channel_id=1, source_target_pairs={{0,64},{16,80},{32,96},{48,112},{64,0},{80,16},{96,32},{112,48},{1... | collective-permute-start | bytes 4718600 | tf_op jit(solution)/shard_map/ppermute | solution.py:13
Sparse Core Ops, SparseCore 0:
  10.7 62.0 all-gather.8
  75.5 44.5 all-gather.4
  125.1 70.1 all-gather.6
